TPU v7x, 512 devices: a whole 4x8x8 slice. The times are simulated.
512 devices in a mesh: segment: 4 (over x), dp: 8 (over y), mp: 16 (over z, core).
Axes of the slice: x: 4, y: 8, z: 8, core: 2. Of those that a mesh axis runs over, the one named last changes fastest.
Arguments:
- pending_inputs: bfloat16 [4, 8192, 4096], P('segment', ('dp', 'mp')), may hold values from -6 to 6
- arriving_samples: bfloat16 [8192, 4096], P(('dp', 'mp')), may hold values from -6 to 6
- layer_rms_gain: float32 [4, 4096], P('segment'), may hold values from 0.25 to 1.75
- scorer_vectors: float32 [4, 4096], P('segment'), may hold values from -0.09375 to 0.09375
- gating_matrix: bfloat16 [4, 4096, 14336], P('segment', 'dp', 'mp'), may hold values from -0.09375 to 0.09375
- expansion_matrix: bfloat16 [4, 4096, 14336], P('segment', 'dp', 'mp'), may hold values from -0.09375 to 0.09375
- contraction_matrix: bfloat16 [4, 14336, 4096], P('segment', 'mp', 'dp'), may hold values from -0.046875 to 0.046875
- dispatch_lists: int32 [2, 4, 128, 8], P(None, 'segment', ('dp', 'mp')), may hold values from -1 to 63, as said below
Outputs:
- first_out: bfloat16 [4, 8192, 4096], P('segment', ('dp', 'mp'))
- second_out: bfloat16 [4, 8192, 4096], P('segment', ('dp', 'mp'))
Inputs may be any that keep to these rules, and one draw needn't show every extreme that they name: `dispatch_lists`: in each list of 8 slots the used slots come first and name distinct rows of the block; the other slots hold -1. Some block of every group of 8 blocks that share an mp index uses all 8 slots, and every such group (same tick and section) uses exactly 32 slots together.
All inputs are finite; a program needn't handle non-finite values.
Results may differ from a plain program's by a relative error of at most 0.0065.
Values may be sent and summed in bfloat16 or wider, within the bound.
No kernel may reach another device: no remote copies, remote signals or barrier semaphores. Data moves between devices by JAX's collectives and lax.ppermute only.
A program may use at most 64 MiB of HBM per device.

v0:
```python
import jax
import jax.numpy as jnp
from jax import lax
from jax.sharding import PartitionSpec as P


def from_behind(value, axis, steps):
    count = lax.axis_size(axis)
    initial, last = (max(0, -steps), min(count, count - steps))
    return lax.ppermute(value, axis, [(source, source + steps) for source in range(initial, last)])


def selection(flags, dense_rows):
    used_slots = (flags[:, 0] > 0).astype(jnp.int32)
    dense_place = jnp.cumsum(used_slots) - 1
    targets = jnp.arange(dense_rows, dtype=jnp.int32)[:, None]
    return ((dense_place[None, :] == targets) & (used_slots[None, :] > 0)).astype(jnp.bfloat16)


def layer_tile(section_in, route_row, gain, router_vec, w_gate_local, w_up_local, w_down_local):
    width_parts = lax.axis_size("dp")
    slot_count = route_row.shape[0]
    is_live = route_row >= 0
    safe_rows = jnp.where(is_live, route_row, 0)
    picked = jnp.take(section_in, safe_rows, axis=0)
    values = picked.astype(jnp.float32)
    inv_rms = lax.rsqrt(jnp.mean(values * values, axis=-1, keepdims=True) + 1e-05)
    normed = jnp.where(is_live[:, None], values * inv_rms * gain, 0.0).astype(jnp.bfloat16)
    live_flags = jnp.broadcast_to(is_live[:, None], (slot_count, width_parts)).astype(jnp.bfloat16)
    slot_rows, flag_col = (
        lax.all_to_all(normed, "dp", split_axis=1, concat_axis=0, tiled=True),
        lax.all_to_all(live_flags, "dp", split_axis=1, concat_axis=0, tiled=True),
    )
    group_rows = width_parts * slot_count // 2
    selector = selection(flag_col, group_rows)
    all_rows, all_flags = (
        lax.all_gather(slot_rows, "mp", axis=0, tiled=True),
        lax.all_gather(flag_col, "mp", axis=0, tiled=True),
    )
    wide_selector = selection(all_flags, lax.axis_size("mp") * group_rows)
    gathered = jnp.dot(wide_selector, all_rows, preferred_element_type=jnp.float32).astype(
        jnp.bfloat16
    )
    joined = jnp.concatenate([w_gate_local, w_up_local], axis=1)
    hidden_cols = w_gate_local.shape[1]
    summed = lax.psum_scatter(
        jnp.dot(gathered, joined, preferred_element_type=jnp.float32).astype(jnp.bfloat16),
        "dp",
        scatter_dimension=0,
        tiled=True,
    ).astype(jnp.float32)
    hidden = (jax.nn.silu(summed[:, :hidden_cols]) * summed[:, hidden_cols:]).astype(jnp.bfloat16)
    all_hidden = lax.all_gather(hidden, "dp", axis=0, tiled=True)
    partial_block = jnp.dot(all_hidden, w_down_local, preferred_element_type=jnp.float32)
    full_sum = lax.psum(partial_block.astype(jnp.bfloat16), "mp").astype(jnp.float32)
    block_out = lax.dynamic_slice_in_dim(full_sum, lax.axis_index("mp") * group_rows, group_rows, 0)
    block_out = block_out.astype(jnp.bfloat16)
    spread_out = jnp.dot(selector.T, block_out, preferred_element_type=jnp.float32).astype(
        jnp.bfloat16
    )
    returned = lax.all_to_all(spread_out, "dp", split_axis=0, concat_axis=1, tiled=True)
    weight = jax.nn.sigmoid(jnp.dot(values, router_vec, precision=lax.Precision.HIGHEST))
    updated = (values + weight[:, None] * returned.astype(jnp.float32)).astype(jnp.bfloat16)
    target = jnp.where(is_live, route_row, section_in.shape[0])
    return section_in.at[target].set(updated, mode="drop")


def local(
    pending_inputs,
    arriving_samples,
    layer_rms_gain,
    scorer_vectors,
    gating_matrix,
    expansion_matrix,
    contraction_matrix,
    dispatch_lists,
):
    first_local = layer_tile(
        pending_inputs[0],
        dispatch_lists[0, 0, 0],
        layer_rms_gain[0],
        scorer_vectors[0],
        gating_matrix[0],
        expansion_matrix[0],
        contraction_matrix[0],
    )
    passed = from_behind(first_local, "segment", 1)
    second_in = jnp.where(lax.axis_index("segment") == 0, arriving_samples, passed)
    second_local = layer_tile(
        second_in,
        dispatch_lists[1, 0, 0],
        layer_rms_gain[0],
        scorer_vectors[0],
        gating_matrix[0],
        expansion_matrix[0],
        contraction_matrix[0],
    )
    return (first_local[None], second_local[None])


def solution(mesh):
    return jax.shard_map(
        local,
        mesh=mesh,
        in_specs=(
            P("segment", ("dp", "mp"), None),
            P(("dp", "mp"), None),
            P("segment", None),
            P("segment", None),
            P("segment", "dp", "mp"),
            P("segment", "dp", "mp"),
            P("segment", "mp", "dp"),
            P(None, "segment", ("dp", "mp"), None),
        ),
        out_specs=(P("segment", ("dp", "mp"), None), P("segment", ("dp", "mp"), None)),
        check_vma=False,
    )
```

profile of v0, /device:TPU:2, one launch (start us, length us, event | category | flops | bytes accessed | tf_op | source)
XLA Modules:
  0.0 563.7 jit_solution(5471080146650865949)
XLA Ops:
  10.7 15.4 %all_to_all.90 = bf16[8,8,512]{2,0,1:T(8,128)(2,1)} all-to-all(bf16[8,8,512]{2,0,1:T(8,128)(2,1)S(1)} %bitcast.119), channel_id=1, replica_groups=mesh['segment'=4,'dp'=8,'mp'=16] {'dp'}, dimensions={1} | all-to-all | bytes 131072 | tf_op jit(solution)/shard_map/all_to_all | solution.py:31
  26.7 3.3 all-to-all-start
  32.0 5.6 all-to-all-done
  38.2 3.3 all-to-all-start.3
  41.6 7.4 %all-to-all-done.3 = bf16[8,8,1]{0,2,1:T(2,128)(2,1)S(1)} async-done(((bf16[8,8,1]{0,2,1:T(2,128)(2,1)}), bf16[8,8,1]{0,2,1:T(2,128)(2,1)S(1)}, u32[]{:S(2)}, u32[]{:S(2)}) %all-to-all-start.3) | async-done | bytes 160 | tf_op jit(solution)/shard_map/all_to_all | solution.py:32
  49.6 29.5 %all-reduce.2 = (bf16[1024]{0:T(1024)(128)(2,1)S(1)}, bf16[1024]{0:T(1024)(128)(2,1)S(1)}) all-reduce(bf16[1024]{0:T(1024)(128)(2,1)S(1)} %dynamic-update-slice, bf16[1024]{0:T(1024)(128)(2,1)S(1)} %dynamic-update-slice.1), channel_id=1, replica_groups=mesh['segment'=4,'dp'=8,'mp'=16] {'mp'}, use_global_device_ids=true, to_apply=%add | all-reduce | flops 2048 | bytes 8192
  79.6 4.6 convolution_convert_fusion.1
  85.2 37.5 %reduce-scatter.3.cloned.1.call-done = bf16[64,1792]{1,0:T(8,128)(2,1)} async-done(((bf16[512,1792]{1,0:T(8,128)(2,1)}), bf16[64,1792]{1,0:T(8,128)(2,1)}) %reduce-scatter.3.cloned.1.call-update) | async-done | bytes 229392 | tf_op jit(solution)/shard_map/reduce_scatter | solution.py:46
  123.8 26.5 %all_gather.20 = bf16[512,896]{1,0:T(8,128)(2,1)S(1)} all-gather(bf16[64,896]{1,0:T(8,128)(2,1)S(1)} %fusion.33), channel_id=1, replica_groups=mesh['segment'=4,'dp'=8,'mp'=16] {'dp'}, dimensions={0}, use_global_device_ids=true | all-gather | bytes 1032192 | tf_op jit(solution)/shard_map/all_gather | solution.py:53
  152.3 114.6 %all-reduce.6.cloned.1.call-done = bf16[512,512]{1,0:T(8,128)(2,1)} async-done(((bf16[512,512]{1,0:T(8,128)(2,1)}), bf16[512,512]{1,0:T(8,128)(2,1)}) %all-reduce.6.cloned.1.call-update) | async-done | bytes 524304 | tf_op jit(solution)/shard_map/psum | solution.py:55
  266.9 1.6 fusion.12
  268.4 6.7 %all-to-all-start.2 = ((bf16[8,8,512]{2,1,0:T(8,128)(2,1)}), bf16[8,8,512]{2,1,0:T(8,128)(2,1)S(1)}, u32[]{:S(2)}, u32[]{:S(2)}) async-start(bf16[8,8,512]{2,1,0:T(8,128)(2,1)} %fusion.12), calls=%async_computation.3 | async-start | bytes 131072 | tf_op jit(solution)/shard_map/all_to_all | solution.py:61
  275.3 8.3 %all-to-all-done.2 = bf16[8,8,512]{2,1,0:T(8,128)(2,1)S(1)} async-done(((bf16[8,8,512]{2,1,0:T(8,128)(2,1)}), bf16[8,8,512]{2,1,0:T(8,128)(2,1)S(1)}, u32[]{:S(2)}, u32[]{:S(2)}) %all-to-all-start.2) | async-done | bytes 65568 | tf_op jit(solution)/shard_map/all_to_all | solution.py:61
  284.7 3.4 collective-permute-start
  288.1 10.7 %collective-permute-done = bf16[64,4096]{1,0:T(8,128)(2,1)S(1)} collective-permute-done((bf16[64,4096]{1,0:T(8,128)(2,1)S(1)}, bf16[64,4096]{1,0:T(8,128)(2,1)S(1)}, u32[]{:S(2)}, u32[]{:S(2)}) %collective-permute-start) | collective-permute-done | bytes 524320 | tf_op jit(solution)/shard_map/ppermute | solution.py:10
  299.8 11.4 %all_to_all.91 = bf16[8,8,512]{2,0,1:T(8,128)(2,1)} all-to-all(bf16[8,8,512]{2,0,1:T(8,128)(2,1)S(1)} %bitcast.120), channel_id=1, replica_groups=mesh['segment'=4,'dp'=8,'mp'=16] {'dp'}, dimensions={1} | all-to-all | bytes 131072 | tf_op jit(solution)/shard_map/all_to_all | solution.py:31
  311.9 35.2 %all-gather.5.cloned.1.call-done = bf16[1024,512]{1,0:T(8,128)(2,1)} async-done(((bf16[64,512]{1,0:T(8,128)(2,1)}), bf16[1024,512]{1,0:T(8,128)(2,1)}) %all-gather.5.cloned.1.call-update) | async-done | bytes 1048592 | tf_op jit(solution)/shard_map/all_gather | solution.py:37
  347.0 4.9 convolution_convert_fusion
  352.0 42.1 %reduce-scatter.5.cloned.1.call-done = bf16[64,1792]{1,0:T(8,128)(2,1)} async-done(((bf16[512,1792]{1,0:T(8,128)(2,1)}), bf16[64,1792]{1,0:T(8,128)(2,1)}) %reduce-scatter.5.cloned.1.call-update) | async-done | bytes 229392 | tf_op jit(solution)/shard_map/reduce_scatter | solution.py:46
  395.2 26.3 %all_gather.23 = bf16[512,896]{1,0:T(8,128)(2,1)S(1)} all-gather(bf16[64,896]{1,0:T(8,128)(2,1)S(1)} %fusion.32), channel_id=1, replica_groups=mesh['segment'=4,'dp'=8,'mp'=16] {'dp'}, dimensions={0}, use_global_device_ids=true | all-gather | bytes 1032192 | tf_op jit(solution)/shard_map/all_gather | solution.py:53
  423.4 114.8 %all-reduce.8.cloned.1.call-done = bf16[512,512]{1,0:T(8,128)(2,1)} async-done(((bf16[512,512]{1,0:T(8,128)(2,1)}), bf16[512,512]{1,0:T(8,128)(2,1)}) %all-reduce.8.cloned.1.call-update) | async-done | bytes 524304 | tf_op jit(solution)/shard_map/psum | solution.py:55
  538.2 1.6 fusion.13
  539.8 6.7 %all-to-all-start.5 = ((bf16[8,8,512]{2,1,0:T(8,128)(2,1)}), bf16[8,8,512]{2,1,0:T(8,128)(2,1)S(1)}, u32[]{:S(2)}, u32[]{:S(2)}) async-start(bf16[8,8,512]{2,1,0:T(8,128)(2,1)} %fusion.13), calls=%async_computation.7 | async-start | bytes 131072 | tf_op jit(solution)/shard_map/all_to_all | solution.py:61
  546.8 8.1 %all-to-all-done.5 = bf16[8,8,512]{2,1,0:T(8,128)(2,1)S(1)} async-done(((bf16[8,8,512]{2,1,0:T(8,128)(2,1)}), bf16[8,8,512]{2,1,0:T(8,128)(2,1)S(1)}, u32[]{:S(2)}, u32[]{:S(2)}) %all-to-all-start.5) | async-done | bytes 65568 | tf_op jit(solution)/shard_map/all_to_all | solution.py:61
  (89 shorter events, 19.2 us)
Async XLA Ops:
  7.2 143.1 %copy-start = (bf16[1,896,512]{2,1,0:T(8,128)(2,1)S(1)}, bf16[1,896,512]{2,1,0:T(8,128)(2,1)}, u32[]{:S(2)}) copy-start(bf16[1,896,512]{2,1,0:T(8,128)(2,1)} %param.16) | copy-start | bytes 2752516
  7.2 72.5 %copy-start.6 = (bf16[1,512,896]{2,1,0:T(8,128)(2,1)S(1)}, bf16[1,512,896]{2,1,0:T(8,128)(2,1)}, u32[]{:S(2)}) copy-start(bf16[1,512,896]{2,1,0:T(8,128)(2,1)} %param.15) | copy-start | bytes 2752516
  7.2 72.4 %all-gather.3.cloned.1.call-start = ((), (), s32[]{:S(2)}) async-start(), calls=%async_computation.8 | async-start | bytes 1114112 | tf_op jit(solution)/shard_map/all_gather | solution.py:37
  26.7 10.8 %all-to-all-start = ((bf16[8,8,1]{0,2,1:T(2,128)(2,1)}), bf16[8,8,1]{0,2,1:T(2,128)(2,1)S(1)}, u32[]{:S(2)}, u32[]{:S(2)}) async-start(bf16[8,8,1]{0,2,1:T(2,128)(2,1)} %broadcast_in_dim.43), calls=%async_computation | async-start | bytes 8192 | tf_op jit(solution)/shard_map/all_to_all | solution.py:32
  38.2 10.8 %all-to-all-start.3 = ((bf16[8,8,1]{0,2,1:T(2,128)(2,1)}), bf16[8,8,1]{0,2,1:T(2,128)(2,1)S(1)}, u32[]{:S(2)}, u32[]{:S(2)}) async-start(bf16[8,8,1]{0,2,1:T(2,128)(2,1)} %broadcast_in_dim.77), calls=%async_computation.4 | async-start | bytes 8192 | tf_op jit(solution)/shard_map/all_to_all | solution.py:32
  41.5 81.3 %reduce-scatter.3.cloned.1.call-start = ((), (), s32[]{:S(2)}) async-start(), calls=%async_computation.9 | async-start | bytes 2064384 | tf_op jit(solution)/shard_map/reduce_scatter | solution.py:46
  84.2 0.7 copy-start.7
  84.2 182.6 %all-reduce.6.cloned.1.call-start = ((), (), s32[]{:S(2)}) async-start(), calls=%async_computation.10 | async-start | bytes 1048576 | tf_op jit(solution)/shard_map/psum | solution.py:55
  150.3 125.0 %copy-start.5 = (s32[2,1,1,8]{3,2,1,0:T(1,128)S(1)}, s32[2,1,1,8]{3,2,1,0:T(1,128)}, u32[]{:S(2)}) copy-start(s32[2,1,1,8]{3,2,1,0:T(1,128)} %param.17) | copy-start | bytes 196
  150.3 148.5 %copy-start.3 = (bf16[64,4096]{1,0:T(8,128)(2,1)S(1)}, bf16[64,4096]{1,0:T(8,128)(2,1)}, u32[]{:S(2)}) copy-start(bf16[64,4096]{1,0:T(8,128)(2,1)} %param.11) | copy-start | bytes 1572868
  151.8 147.9 %copy-start.4 = (f32[1,4096]{1,0:T(1,128)S(1)}, f32[1,4096]{1,0:T(1,128)}, u32[]{:S(2)}) copy-start(f32[1,4096]{1,0:T(1,128)} %param.12) | copy-start | bytes 49156
  268.4 15.1 %all-to-all-start.2 = ((bf16[8,8,512]{2,1,0:T(8,128)(2,1)}), bf16[8,8,512]{2,1,0:T(8,128)(2,1)S(1)}, u32[]{:S(2)}, u32[]{:S(2)}) async-start(bf16[8,8,512]{2,1,0:T(8,128)(2,1)} %fusion.12), calls=%async_computation.3 | async-start | bytes 131072 | tf_op jit(solution)/shard_map/all_to_all | solution.py:61
  275.2 71.9 %all-gather.5.cloned.1.call-start = ((), (), s32[]{:S(2)}) async-start(), calls=%async_computation.11 | async-start | bytes 1114112 | tf_op jit(solution)/shard_map/all_gather | solution.py:37
  284.7 67.2 %copy-start.1 = (bf16[64,4096]{1,0:T(8,128)(2,1)}, bf16[64,4096]{1,0:T(8,128)(2,1)S(1)}, u32[]{:S(2)}) copy-start(bf16[64,4096]{1,0:T(8,128)(2,1)S(1)} %scatter_custom_fusion) | copy-start | bytes 1572868
  284.7 14.1 %collective-permute-start = (bf16[64,4096]{1,0:T(8,128)(2,1)S(1)}, bf16[64,4096]{1,0:T(8,128)(2,1)S(1)}, u32[]{:S(2)}, u32[]{:S(2)}) collective-permute-start(bf16[64,4096]{1,0:T(8,128)(2,1)S(1)} %scatter_custom_fusion), channel_id=1, source_target_pairs={{0,128},{128,256},{256,384},{1,129},{129,257},{257,385},{2,130},{1... | collective-permute-start | bytes 1572872 | tf_op jit(solution)/shard_map/ppermute | solution.py:10
  311.2 82.9 %reduce-scatter.5.cloned.1.call-start = ((), (), s32[]{:S(2)}) async-start(), calls=%async_computation.12 | async-start | bytes 2064384 | tf_op jit(solution)/shard_map/reduce_scatter | solution.py:46
  351.9 186.3 %all-reduce.8.cloned.1.call-start = ((), (), s32[]{:S(2)}) async-start(), calls=%async_computation.13 | async-start | bytes 1048576 | tf_op jit(solution)/shard_map/psum | solution.py:55
  539.8 15.1 %all-to-all-start.5 = ((bf16[8,8,512]{2,1,0:T(8,128)(2,1)}), bf16[8,8,512]{2,1,0:T(8,128)(2,1)S(1)}, u32[]{:S(2)}, u32[]{:S(2)}) async-start(bf16[8,8,512]{2,1,0:T(8,128)(2,1)} %fusion.13), calls=%async_computation.7 | async-start | bytes 131072 | tf_op jit(solution)/shard_map/all_to_all | solution.py:61
  556.0 0.8 copy-start.2
Sparse Core Ops, SparseCore 0:
  26.3 41.3 all-gather.2
  84.4 38.3 reduce-scatter.2
  151.9 114.8 all-reduce.5
  311.4 35.6 all-gather.4
  352.1 42.0 reduce-scatter.4
  423.2 115.0 all-reduce.7
where the time goes:
time: 565 us; the launch traced here: 564 us
  waiting for transfers between devices  384 us (68%)
  blocking collectives  109 us (19%)
  starting transfers between devices  23.7 us (4%)
  matrix products  16.2 us (3%)
  between operations  15 us (3%)
  other arithmetic  7.69 us (1%)
  local copies, waits for them, and re-layouts  7.64 us (1%)
    psum x2, waiting for transfers between devices, layer_tile(): lax.psum(partial_block.astype(jnp.bfloat16), 'mp').astype(jnp.float32)  229 us
    reduce_scatter x2, waiting for transfers between devices, layer_tile(): lax.psum_scatter(jnp.dot(gathered, joined, preferred_element_type=jnp.flo...  79.7 us
    all_gather x2, blocking collectives, layer_tile(): all_hidden = lax.all_gather(hidden, 'dp', axis=0, tiled=True)  52.8 us
    all_gather x2, waiting for transfers between devices, layer_tile(): lax.all_gather(slot_rows, 'mp', axis=0, tiled=True)  35.2 us
    unnamed x1, blocking collectives  29.5 us
    all_to_all x2, blocking collectives, layer_tile(): lax.all_to_all(normed, 'dp', split_axis=1, concat_axis=0, tiled=True)  26.8 us
    all_to_all x2, waiting for transfers between devices, layer_tile(): lax.all_to_all(spread_out, 'dp', split_axis=0, concat_axis=1, tiled=True)  16.4 us
    all_to_all x2, starting transfers between devices, layer_tile(): lax.all_to_all(spread_out, 'dp', split_axis=0, concat_axis=1, tiled=True)  13.5 us
  transfers between devices with their start and end apart: 11, of which 10 were waited for; matrix products, arithmetic and copies ran while one was open for 1% of the time, Pallas kernels for 0%

commit v1 on v0

--- a/solution.py
+++ b/solution.py
@@ -52,7 +52,9 @@
     hidden = (jax.nn.silu(summed[:, :hidden_cols]) * summed[:, hidden_cols:]).astype(jnp.bfloat16)
     all_hidden = lax.all_gather(hidden, "dp", axis=0, tiled=True)
     partial_block = jnp.dot(all_hidden, w_down_local, preferred_element_type=jnp.float32)
-    full_sum = lax.psum(partial_block.astype(jnp.bfloat16), "mp").astype(jnp.float32)
+    full_sum = jnp.sum(lax.all_gather(partial_block.astype(jnp.bfloat16), "mp"), axis=0).astype(
+        jnp.float32
+    )
     block_out = lax.dynamic_slice_in_dim(full_sum, lax.axis_index("mp") * group_rows, group_rows, 0)
     block_out = block_out.astype(jnp.bfloat16)
     spread_out = jnp.dot(selector.T, block_out, preferred_element_type=jnp.float32).astype(

time: 565 us -> 459 us (0.81)
  waiting for transfers between devices: 384 us -> 272 us
  other arithmetic: 7.69 us -> 17.4 us
    psum x2 -> x0, waiting for transfers between devices: 229 us -> none  [layer_tile(): lax.psum(partial_block.astype(jnp.bfloat16), 'mp').astype(jnp.float32)]
    all_gather x0 -> x2, waiting for transfers between devices: none -> 116 us  [layer_tile(): lax.all_gather(partial_block.astype(jnp.bfloat16), 'mp')]
    reduce_sum x0 -> x2, other arithmetic: none -> 9.7 us  [layer_tile(): jnp.sum(lax.all_gather(partial_block.astype(jnp.bfloat16), 'mp'), axis=0)]
where the time goes in v1:
time: 459 us
  waiting for transfers between devices  272 us (59%)
  blocking collectives  109 us (24%)
  starting transfers between devices  23.7 us (5%)
  other arithmetic  17.4 us (4%)
  between operations  15 us (3%)
  matrix products  14.7 us (3%)
  local copies, waits for them, and re-layouts  7 us (2%)
    all_gather x2, waiting for transfers between devices, layer_tile(): lax.all_gather(partial_block.astype(jnp.bfloat16), 'mp')  116 us
    reduce_scatter x2, waiting for transfers between devices, layer_tile(): lax.psum_scatter(jnp.dot(gathered, joined, preferred_element_type=jnp.flo...  80.6 us
    all_gather x2, blocking collectives, layer_tile(): all_hidden = lax.all_gather(hidden, 'dp', axis=0, tiled=True)  52.9 us
    all_gather x2, waiting for transfers between devices, layer_tile(): lax.all_gather(slot_rows, 'mp', axis=0, tiled=True)  34.6 us
    unnamed x1, blocking collectives  29.5 us
    all_to_all x2, blocking collectives, layer_tile(): lax.all_to_all(normed, 'dp', split_axis=1, concat_axis=0, tiled=True)  26.8 us
    all_to_all x2, waiting for transfers between devices, layer_tile(): lax.all_to_all(spread_out, 'dp', split_axis=0, concat_axis=1, tiled=True)  16.4 us
    all_to_all x2, starting transfers between devices, layer_tile(): lax.all_to_all(spread_out, 'dp', split_axis=0, concat_axis=1, tiled=True)  13.5 us
  transfers between devices with their start and end apart: 11, of which 10 were waited for; matrix products, arithmetic and copies ran while one was open for 1% of the time, Pallas kernels for 0%

profile of v1, /device:TPU:2, one launch (start us, length us, event | category | flops | bytes accessed | tf_op | source)
XLA Modules:
  0.0 458.7 jit_solution(14467502710501556225)
XLA Ops:
  10.7 15.4 %all_to_all.90 = bf16[8,8,512]{2,0,1:T(8,128)(2,1)} all-to-all(bf16[8,8,512]{2,0,1:T(8,128)(2,1)S(1)} %bitcast.123), channel_id=1, replica_groups=mesh['segment'=4,'dp'=8,'mp'=16] {'dp'}, dimensions={1} | all-to-all | bytes 131072 | tf_op jit(solution)/shard_map/all_to_all | solution.py:31
  26.7 3.3 all-to-all-start
  32.0 5.6 %all-to-all-done = bf16[8,8,1]{0,2,1:T(2,128)(2,1)S(1)} async-done(((bf16[8,8,1]{0,2,1:T(2,128)(2,1)}), bf16[8,8,1]{0,2,1:T(2,128)(2,1)S(1)}, u32[]{:S(2)}, u32[]{:S(2)}) %all-to-all-start) | async-done | bytes 160 | tf_op jit(solution)/shard_map/all_to_all | solution.py:32
  38.2 3.3 all-to-all-start.3
  41.6 7.4 %all-to-all-done.3 = bf16[8,8,1]{0,2,1:T(2,128)(2,1)S(1)} async-done(((bf16[8,8,1]{0,2,1:T(2,128)(2,1)}), bf16[8,8,1]{0,2,1:T(2,128)(2,1)S(1)}, u32[]{:S(2)}, u32[]{:S(2)}) %all-to-all-start.3) | async-done | bytes 160 | tf_op jit(solution)/shard_map/all_to_all | solution.py:32
  49.6 29.5 %all-reduce.2 = (bf16[1024]{0:T(1024)(128)(2,1)S(1)}, bf16[1024]{0:T(1024)(128)(2,1)S(1)}) all-reduce(bf16[1024]{0:T(1024)(128)(2,1)S(1)} %dynamic-update-slice, bf16[1024]{0:T(1024)(128)(2,1)S(1)} %dynamic-update-slice.1), channel_id=1, replica_groups=mesh['segment'=4,'dp'=8,'mp'=16] {'mp'}, use_global_device_ids=true, to_apply=%add | all-reduce | flops 2048 | bytes 8192
  79.6 4.6 %convolution_convert_fusion.1 = bf16[512,1792]{1,0:T(8,128)(2,1)} fusion(bf16[512,896]{1,0:T(8,128)(2,1)S(1)} %bitcast.130, bf16[512,896]{1,0:T(8,128)(2,1)} %bitcast.131, bf16[1024,512]{1,0:T(8,128)(2,1)} %all-gather.7.cloned.1.call-done, s32[1024]{0:T(1024)S(1)} %add_bitcast_fusion.1, pred[1024]{0:T(1024)(128)(4,1)S(1)} %get-tuple-element.11), kind=kOutput, calls=%fused_computation.5 | convolution fusion | flops 1482293248 | bytes 4723712 | tf_op jit(solution)/shard_map/dot_general | solution.py:47
  84.3 38.5 %reduce-scatter.3.cloned.1.call-done = bf16[64,1792]{1,0:T(8,128)(2,1)} async-done(((bf16[512,1792]{1,0:T(8,128)(2,1)}), bf16[64,1792]{1,0:T(8,128)(2,1)}) %reduce-scatter.3.cloned.1.call-update) | async-done | bytes 229392 | tf_op jit(solution)/shard_map/reduce_scatter | solution.py:46
  123.8 26.5 %all_gather.32 = bf16[512,896]{1,0:T(8,128)(2,1)S(1)} all-gather(bf16[64,896]{1,0:T(8,128)(2,1)S(1)} %fusion.33), channel_id=1, replica_groups=mesh['segment'=4,'dp'=8,'mp'=16] {'dp'}, dimensions={0}, use_global_device_ids=true | all-gather | bytes 1032192 | tf_op jit(solution)/shard_map/all_gather | solution.py:53
  152.6 57.7 %all-gather.11.cloned.1.call-done = bf16[8192,512]{1,0:T(8,128)(2,1)} async-done(((bf16[512,512]{1,0:T(8,128)(2,1)}), bf16[8192,512]{1,0:T(8,128)(2,1)}) %all-gather.11.cloned.1.call-update) | async-done | bytes 8388624 | tf_op jit(solution)/shard_map/all_gather | solution.py:55
  210.3 4.9 %reduce_sum.43 = bf16[512,512]{1,0:T(8,128)(2,1)S(1)} reduce(bf16[16,512,512]{2,1,0:T(8,128)(2,1)} %bitcast.115, bf16[]{:T(256)} %constant.32.clone.1), dimensions={0}, to_apply=%region_5.7 | reduce | flops 3932160 | bytes 8912898 | tf_op jit(solution)/shard_map/reduce_sum | solution.py:55
  216.1 6.7 %all-to-all-start.2 = ((bf16[8,8,512]{2,1,0:T(8,128)(2,1)}), bf16[8,8,512]{2,1,0:T(8,128)(2,1)S(1)}, u32[]{:S(2)}, u32[]{:S(2)}) async-start(bf16[8,8,512]{2,1,0:T(8,128)(2,1)} %fusion.12), calls=%async_computation.3 | async-start | bytes 131072 | tf_op jit(solution)/shard_map/all_to_all | solution.py:63
  222.9 8.3 %all-to-all-done.2 = bf16[8,8,512]{2,1,0:T(8,128)(2,1)S(1)} async-done(((bf16[8,8,512]{2,1,0:T(8,128)(2,1)}), bf16[8,8,512]{2,1,0:T(8,128)(2,1)S(1)}, u32[]{:S(2)}, u32[]{:S(2)}) %all-to-all-start.2) | async-done | bytes 65568 | tf_op jit(solution)/shard_map/all_to_all | solution.py:63
  232.3 3.4 collective-permute-start
  235.7 11.1 %collective-permute-done = bf16[64,4096]{1,0:T(8,128)(2,1)S(1)} collective-permute-done((bf16[64,4096]{1,0:T(8,128)(2,1)S(1)}, bf16[64,4096]{1,0:T(8,128)(2,1)S(1)}, u32[]{:S(2)}, u32[]{:S(2)}) %collective-permute-start) | collective-permute-done | bytes 524320 | tf_op jit(solution)/shard_map/ppermute | solution.py:10
  247.8 11.4 %all_to_all.91 = bf16[8,8,512]{2,0,1:T(8,128)(2,1)} all-to-all(bf16[8,8,512]{2,0,1:T(8,128)(2,1)S(1)} %bitcast.124), channel_id=1, replica_groups=mesh['segment'=4,'dp'=8,'mp'=16] {'dp'}, dimensions={1} | all-to-all | bytes 131072 | tf_op jit(solution)/shard_map/all_to_all | solution.py:31
  259.9 34.6 %all-gather.9.cloned.1.call-done = bf16[1024,512]{1,0:T(8,128)(2,1)} async-done(((bf16[64,512]{1,0:T(8,128)(2,1)}), bf16[1024,512]{1,0:T(8,128)(2,1)}) %all-gather.9.cloned.1.call-update) | async-done | bytes 1048592 | tf_op jit(solution)/shard_map/all_gather | solution.py:37
  294.5 4.9 %convolution_convert_fusion = bf16[512,1792]{1,0:T(8,128)(2,1)} fusion(bf16[512,896]{1,0:T(8,128)(2,1)} %bitcast.129, bf16[512,896]{1,0:T(8,128)(2,1)} %bitcast.132, bf16[1024,512]{1,0:T(8,128)(2,1)} %all-gather.9.cloned.1.call-done, s32[1024]{0:T(1024)S(1)} %add_bitcast_fusion, pred[1024]{0:T(1024)(128)(4,1)S(1)} %get-tuple-element.9), kind=kOutput, calls=%fused_computation.4 | convolution fusion | flops 1482293248 | bytes 4723712 | tf_op jit(solution)/shard_map/dot_general | solution.py:47
  299.5 42.2 %reduce-scatter.5.cloned.1.call-done = bf16[64,1792]{1,0:T(8,128)(2,1)} async-done(((bf16[512,1792]{1,0:T(8,128)(2,1)}), bf16[64,1792]{1,0:T(8,128)(2,1)}) %reduce-scatter.5.cloned.1.call-update) | async-done | bytes 229392 | tf_op jit(solution)/shard_map/reduce_scatter | solution.py:46
  342.7 26.4 %all_gather.37 = bf16[512,896]{1,0:T(8,128)(2,1)S(1)} all-gather(bf16[64,896]{1,0:T(8,128)(2,1)S(1)} %fusion.32), channel_id=1, replica_groups=mesh['segment'=4,'dp'=8,'mp'=16] {'dp'}, dimensions={0}, use_global_device_ids=true | all-gather | bytes 1032192 | tf_op jit(solution)/shard_map/all_gather | solution.py:53
  371.0 58.2 %all-gather.13.cloned.1.call-done = bf16[8192,512]{1,0:T(8,128)(2,1)} async-done(((bf16[512,512]{1,0:T(8,128)(2,1)}), bf16[8192,512]{1,0:T(8,128)(2,1)}) %all-gather.13.cloned.1.call-update) | async-done | bytes 8388624 | tf_op jit(solution)/shard_map/all_gather | solution.py:55
  429.1 4.8 %reduce_sum.45 = bf16[512,512]{1,0:T(8,128)(2,1)S(1)} reduce(bf16[16,512,512]{2,1,0:T(8,128)(2,1)} %bitcast.116, bf16[]{:T(256)} %constant.32.clone.1), dimensions={0}, to_apply=%region_12.14 | reduce | flops 3932160 | bytes 8912898 | tf_op jit(solution)/shard_map/reduce_sum | solution.py:55
  434.8 6.7 %all-to-all-start.5 = ((bf16[8,8,512]{2,1,0:T(8,128)(2,1)}), bf16[8,8,512]{2,1,0:T(8,128)(2,1)S(1)}, u32[]{:S(2)}, u32[]{:S(2)}) async-start(bf16[8,8,512]{2,1,0:T(8,128)(2,1)} %fusion.13), calls=%async_computation.7 | async-start | bytes 131072 | tf_op jit(solution)/shard_map/all_to_all | solution.py:63
  441.8 8.1 %all-to-all-done.5 = bf16[8,8,512]{2,1,0:T(8,128)(2,1)S(1)} async-done(((bf16[8,8,512]{2,1,0:T(8,128)(2,1)}), bf16[8,8,512]{2,1,0:T(8,128)(2,1)S(1)}, u32[]{:S(2)}, u32[]{:S(2)}) %all-to-all-start.5) | async-done | bytes 65568 | tf_op jit(solution)/shard_map/all_to_all | solution.py:63
  (91 shorter events, 20.4 us)
Async XLA Ops:
  7.2 143.2 %copy-start = (bf16[1,896,512]{2,1,0:T(8,128)(2,1)S(1)}, bf16[1,896,512]{2,1,0:T(8,128)(2,1)}, u32[]{:S(2)}) copy-start(bf16[1,896,512]{2,1,0:T(8,128)(2,1)} %param.16) | copy-start | bytes 2752516
  7.2 72.5 %copy-start.6 = (bf16[1,512,896]{2,1,0:T(8,128)(2,1)S(1)}, bf16[1,512,896]{2,1,0:T(8,128)(2,1)}, u32[]{:S(2)}) copy-start(bf16[1,512,896]{2,1,0:T(8,128)(2,1)} %param.15) | copy-start | bytes 2752516
  7.2 72.4 %all-gather.7.cloned.1.call-start = ((), (), s32[]{:S(2)}) async-start(), calls=%async_computation.8 | async-start | bytes 1114112 | tf_op jit(solution)/shard_map/all_gather | solution.py:37
  26.7 10.8 %all-to-all-start = ((bf16[8,8,1]{0,2,1:T(2,128)(2,1)}), bf16[8,8,1]{0,2,1:T(2,128)(2,1)S(1)}, u32[]{:S(2)}, u32[]{:S(2)}) async-start(bf16[8,8,1]{0,2,1:T(2,128)(2,1)} %broadcast_in_dim.43), calls=%async_computation | async-start | bytes 8192 | tf_op jit(solution)/shard_map/all_to_all | solution.py:32
  38.2 10.8 %all-to-all-start.3 = ((bf16[8,8,1]{0,2,1:T(2,128)(2,1)}), bf16[8,8,1]{0,2,1:T(2,128)(2,1)S(1)}, u32[]{:S(2)}, u32[]{:S(2)}) async-start(bf16[8,8,1]{0,2,1:T(2,128)(2,1)} %broadcast_in_dim.77), calls=%async_computation.4 | async-start | bytes 8192 | tf_op jit(solution)/shard_map/all_to_all | solution.py:32
  41.5 81.3 %reduce-scatter.3.cloned.1.call-start = ((), (), s32[]{:S(2)}) async-start(), calls=%async_computation.9 | async-start | bytes 2064384 | tf_op jit(solution)/shard_map/reduce_scatter | solution.py:46
  84.3 126.1 %all-gather.11.cloned.1.call-start = ((), (), s32[]{:S(2)}) async-start(), calls=%async_computation.12 | async-start | bytes 8912896 | tf_op jit(solution)/shard_map/all_gather | solution.py:55
  123.8 28.0 %copy-start.7 = (f32[1,4096]{1,0:T(1,128)S(1)}, f32[1,4096]{1,0:T(1,128)}, u32[]{:S(2)}) copy-start(f32[1,4096]{1,0:T(1,128)} %param.13) | copy-start | bytes 49156
  210.3 12.5 %copy-start.5 = (s32[2,1,1,8]{3,2,1,0:T(1,128)S(1)}, s32[2,1,1,8]{3,2,1,0:T(1,128)}, u32[]{:S(2)}) copy-start(s32[2,1,1,8]{3,2,1,0:T(1,128)} %param.17) | copy-start | bytes 196
  210.3 36.5 %copy-start.3 = (bf16[64,4096]{1,0:T(8,128)(2,1)S(1)}, bf16[64,4096]{1,0:T(8,128)(2,1)}, u32[]{:S(2)}) copy-start(bf16[64,4096]{1,0:T(8,128)(2,1)} %param.11) | copy-start | bytes 1572868
  215.2 32.5 %copy-start.4 = (f32[1,4096]{1,0:T(1,128)S(1)}, f32[1,4096]{1,0:T(1,128)}, u32[]{:S(2)}) copy-start(f32[1,4096]{1,0:T(1,128)} %param.12) | copy-start | bytes 49156
  216.1 15.1 %all-to-all-start.2 = ((bf16[8,8,512]{2,1,0:T(8,128)(2,1)}), bf16[8,8,512]{2,1,0:T(8,128)(2,1)S(1)}, u32[]{:S(2)}, u32[]{:S(2)}) async-start(bf16[8,8,512]{2,1,0:T(8,128)(2,1)} %fusion.12), calls=%async_computation.3 | async-start | bytes 131072 | tf_op jit(solution)/shard_map/all_to_all | solution.py:63
  222.8 71.7 %all-gather.9.cloned.1.call-start = ((), (), s32[]{:S(2)}) async-start(), calls=%async_computation.10 | async-start | bytes 1114112 | tf_op jit(solution)/shard_map/all_gather | solution.py:37
  232.3 67.1 %copy-start.1 = (bf16[64,4096]{1,0:T(8,128)(2,1)}, bf16[64,4096]{1,0:T(8,128)(2,1)S(1)}, u32[]{:S(2)}) copy-start(bf16[64,4096]{1,0:T(8,128)(2,1)S(1)} %scatter_custom_fusion) | copy-start | bytes 1572868
  232.3 14.5 %collective-permute-start = (bf16[64,4096]{1,0:T(8,128)(2,1)S(1)}, bf16[64,4096]{1,0:T(8,128)(2,1)S(1)}, u32[]{:S(2)}, u32[]{:S(2)}) collective-permute-start(bf16[64,4096]{1,0:T(8,128)(2,1)S(1)} %scatter_custom_fusion), channel_id=1, source_target_pairs={{0,128},{128,256},{256,384},{1,129},{129,257},{257,385},{2,130},{1... | collective-permute-start | bytes 1572872 | tf_op jit(solution)/shard_map/ppermute | solution.py:10
  259.3 82.3 %reduce-scatter.5.cloned.1.call-start = ((), (), s32[]{:S(2)}) async-start(), calls=%async_computation.11 | async-start | bytes 2064384 | tf_op jit(solution)/shard_map/reduce_scatter | solution.py:46
  299.4 129.7 %all-gather.13.cloned.1.call-start = ((), (), s32[]{:S(2)}) async-start(), calls=%async_computation.13 | async-start | bytes 8912896 | tf_op jit(solution)/shard_map/all_gather | solution.py:55
  434.8 15.1 %all-to-all-start.5 = ((bf16[8,8,512]{2,1,0:T(8,128)(2,1)}), bf16[8,8,512]{2,1,0:T(8,128)(2,1)S(1)}, u32[]{:S(2)}, u32[]{:S(2)}) async-start(bf16[8,8,512]{2,1,0:T(8,128)(2,1)} %fusion.13), calls=%async_computation.7 | async-start | bytes 131072 | tf_op jit(solution)/shard_map/all_to_all | solution.py:63
  451.1 0.8 copy-start.2
Sparse Core Ops, SparseCore 0:
  26.3 41.3 all-gather.6
  84.4 38.3 reduce-scatter.2
  152.0 58.2 all-gather.10
  259.4 35.0 all-gather.8
  299.5 42.0 reduce-scatter.4
  370.7 58.4 all-gather.12
